TPU v7x, 512 devices: a whole 4x8x8 slice. The times are simulated.
512 devices in a mesh: dp: 16 (over x_lo, y), fsdp: 32 (over z, x_hi, core).
Axes of the slice: x: 4 (x_hi: 2, x_lo: 2; x = x_hi * 2 + x_lo), y: 8, z: 8, core: 2. Of those that a mesh axis runs over, the one named last changes fastest.
Arguments:
- acts: bfloat16 [8192, 32768], P('fsdp', 'dp'), may hold values from -6 to 6
- grads: bfloat16 [32768, 14336], P('dp', 'fsdp'), may hold values from -0.01953125 to 0.01953125
- basis: bfloat16 [8192, 512], P('fsdp'), may hold values from -0.625 to 0.625
- moment: float32 [512, 14336], P('dp', 'fsdp'), may hold values from -3 to 3
- second: float32 [512, 14336], P('dp', 'fsdp'), may hold values from 0.05 to 1
Outputs:
- moment_new: float32 [512, 14336], P('dp', 'fsdp')
- second_new: float32 [512, 14336], P('dp', 'fsdp')
- dense_update: bfloat16 [8192, 14336], P('fsdp', 'dp')
All inputs are finite; a program needn't handle non-finite values.
Results may differ from a plain program's by a relative error of at most 0.019.
Values may be sent and summed in bfloat16 or wider, within the bound.
A program may use at most 64 MiB of HBM per device.

v0:
```python
import jax
import jax.numpy as jnp
from jax import lax
from jax.sharding import PartitionSpec as P


def shards(acts, grads, basis, moment, second):
    partial_proj = lax.dot_general(
        acts, basis, (((0,), (0,)), ((), ())), preferred_element_type=jnp.float32
    )
    whole_proj = lax.psum(partial_proj.astype(jnp.bfloat16), "fsdp")
    low_partial = lax.dot_general(
        whole_proj, grads, (((0,), (0,)), ((), ())), preferred_element_type=jnp.float32
    )
    low_grad = lax.psum_scatter(
        low_partial.astype(jnp.bfloat16), "dp", scatter_dimension=0, tiled=True
    ).astype(jnp.float32)
    moment_new = 0.9 * moment + 0.1 * low_grad
    second_new = 0.95 * second + 0.05 * low_grad * low_grad
    step_dir = (moment_new / (jnp.sqrt(second_new) + 1e-08)).astype(jnp.bfloat16)
    all_columns = lax.all_gather(step_dir, "fsdp", axis=1, tiled=True)
    all_ranks = lax.all_to_all(all_columns, "dp", split_axis=1, concat_axis=0, tiled=True)
    dense_update = jnp.dot(basis, all_ranks, preferred_element_type=jnp.float32).astype(
        jnp.bfloat16
    )
    return (moment_new, second_new, dense_update)


def solution(mesh):
    in_specs = (P("fsdp", "dp"), P("dp", "fsdp"), P("fsdp", None), P("dp", "fsdp"), P("dp", "fsdp"))
    out_specs = (P("dp", "fsdp"), P("dp", "fsdp"), P("fsdp", "dp"))
    return jax.shard_map(shards, mesh=mesh, in_specs=in_specs, out_specs=out_specs, check_vma=False)
```

profile of v0, /device:TPU:7, one launch (start us, length us, event | category | flops | bytes accessed | tf_op | source)
XLA Modules:
  0.0 450.7 jit_solution(14416530389569607102)
XLA Ops:
  7.2 0.0 copy-start
  7.2 0.0 all-reduce.2.cloned.1.call-start
  7.2 3.4 convolution_convert_fusion
  10.7 0.0 all-reduce.2.cloned.1.call-update
  10.7 0.0 copy-start.2
  10.7 0.0 copy-start.3
  10.7 0.0 reduce-scatter.2.cloned.1.call-start
  10.8 280.2 %all-reduce.2.cloned.1.call-done = bf16[2048,512]{1,0:T(8,128)(2,1)} async-done(((bf16[2048,512]{1,0:T(8,128)(2,1)}), bf16[2048,512]{1,0:T(8,128)(2,1)}) %all-reduce.2.cloned.1.call-update) | async-done | bytes 2097168 | tf_op jit(solution)/shard_map/psum | solution.py:11
  291.0 0.0 copy-done
  291.0 3.7 convolution_convert_fusion.1
  294.7 0.0 reduce-scatter.2.cloned.1.call-update
  294.7 63.8 %reduce-scatter.2.cloned.1.call-done = bf16[32,448]{1,0:T(8,128)(2,1)} async-done(((bf16[512,448]{1,0:T(8,128)(2,1)}), bf16[32,448]{1,0:T(8,128)(2,1)}) %reduce-scatter.2.cloned.1.call-update) | async-done | bytes 28688 | tf_op jit(solution)/shard_map/reduce_scatter | solution.py:15
  358.4 0.0 copy-done.2
  358.5 0.0 copy-done.3
  358.5 1.4 fusion.3
  359.9 53.6 %all-gather = bf16[32,448,32]{1,2,0:T(8,128)(2,1)S(1)} all-gather(bf16[1,448,32]{1,2,0:T(8,128)(2,1)S(1)} %get-tuple-element.12), channel_id=1, replica_groups=mesh['dp'=16,'fsdp'=32] {'fsdp'}, dimensions={0}, use_global_device_ids=true | all-gather | bytes 946176 | tf_op jit(solution)/shard_map/all_gather | solution.py:21
  413.5 0.6 copy.12
  414.1 2.1 reshape.10
  416.2 0.0 copy-start.1
  416.2 1.3 copy.17
  417.5 24.9 %all_to_all.19 = bf16[32,16,896]{2,0,1:T(8,128)(2,1)S(1)} all-to-all(bf16[32,16,896]{2,0,1:T(8,128)(2,1)S(1)} %bitcast.22), channel_id=1, replica_groups=mesh['dp'=16,'fsdp'=32] {'dp'}, dimensions={1} | all-to-all | bytes 1835008 | tf_op jit(solution)/shard_map/all_to_all | solution.py:22
  442.4 0.0 copy-done.1
  442.4 0.4 fusion
  442.9 1.0 copy.14
Async XLA Ops:
  7.2 283.8 %copy-start = (bf16[2048,448]{0,1:T(8,128)(2,1)S(1)}, bf16[2048,448]{0,1:T(8,128)(2,1)}, u32[]{:S(2)}) copy-start(bf16[2048,448]{0,1:T(8,128)(2,1)} %param.6) | copy-start | bytes 5505028
  7.2 283.8 %all-reduce.2.cloned.1.call-start = ((), (), s32[]{:S(2)}) async-start(), calls=%async_computation.2 | async-start | bytes 4194304 | tf_op jit(solution)/shard_map/psum | solution.py:11
  10.7 347.8 %copy-start.2 = (f32[32,448]{1,0:T(8,128)S(1)}, f32[32,448]{1,0:T(8,128)}, u32[]{:S(2)}) copy-start(f32[32,448]{1,0:T(8,128)} %param.9) | copy-start | bytes 172036
  10.7 347.8 %copy-start.3 = (f32[32,448]{1,0:T(8,128)S(1)}, f32[32,448]{1,0:T(8,128)}, u32[]{:S(2)}) copy-start(f32[32,448]{1,0:T(8,128)} %param.8) | copy-start | bytes 172036
  10.7 347.7 %reduce-scatter.2.cloned.1.call-start = ((), (), s32[]{:S(2)}) async-start(), calls=%async_computation.3 | async-start | bytes 557056 | tf_op jit(solution)/shard_map/reduce_scatter | solution.py:15
  416.2 26.2 %copy-start.1 = (bf16[256,512]{1,0:T(8,128)(2,1)S(1)}, bf16[256,512]{1,0:T(8,128)(2,1)}, u32[]{:S(2)}) copy-start(bf16[256,512]{1,0:T(8,128)(2,1)} %param.7) | copy-start | bytes 786436
Sparse Core Ops, SparseCore 0:
  10.9 280.0 all-reduce.1
  294.8 63.5 reduce-scatter.1
where the time goes:
time: 458 us; the launch traced here: 451 us
  waiting for transfers between devices  344 us (75%)
  blocking collectives  78.5 us (17%)
  between operations  14.1 us (3%)
  matrix products  7.56 us (2%)
  local copies, waits for them, and re-layouts  5 us (1%)
    psum x1, waiting for transfers between devices, shards(): whole_proj = lax.psum(partial_proj.astype(jnp.bfloat16), 'fsdp')  280 us
    reduce_scatter x1, waiting for transfers between devices, shards(): lax.psum_scatter(low_partial.astype(jnp.bfloat16), 'dp', scatter_dimensio...  63.8 us
    all_gather x1, blocking collectives, shards(): all_columns = lax.all_gather(step_dir, 'fsdp', axis=1, tiled=True)  53.6 us
    all_to_all x1, blocking collectives, shards(): lax.all_to_all(all_columns, 'dp', split_axis=1, concat_axis=0, tiled=True)  24.9 us
  transfers between devices with their start and end apart: 2, of which 2 were waited for; matrix products, arithmetic and copies ran while one was open for 0% of the time, Pallas kernels for 0%

commit v1 on v0

v1 whole, which is shorter than its diff:
```python
import jax
import jax.numpy as jnp
from jax import lax
from jax.experimental import pallas as pl
from jax.experimental.pallas import tpu as pltpu
from jax.sharding import PartitionSpec as P

F32 = jnp.float32
BF16 = jnp.bfloat16
MESH = pl.DeviceIdType.MESH
TOK = 256
HALF = 256
Q = 128
COLS = 448
ROWS = 32

CORE = 0
RING = 8
XHI = 22
GATH = 24
SHARE = 38
DPX = 54
TRAN = 70
STEP = 72
SHST = 80
COUNT = 89


def kernel(
    acts, basis, grads_hbm, moment, second,
    moment_new, second_new, dense,
    grads, own, csend, crecv, rsend, rrecv, xsend, xrecv, proj, acc, low, lowr, step, steps,
    local_sem, ss, rs,
):
    dp, fs = lax.axis_index("dp"), lax.axis_index("fsdp")
    xl, y = dp // 8, dp % 8
    z, h, c = fs // 4, (fs // 2) % 2, fs % 2

    def at(dz=0, dh=0, dc=0):
        return (dp, ((z + dz + 8) % 8) * 4 + ((h + dh) % 2) * 2 + (c + dc) % 2)

    def dp_at(dx, dy):
        return (((xl + dx) % 2) * 8 + (y + dy) % 8, fs)

    def copy(src, dst, number, device):
        return pltpu.make_async_remote_copy(
            src_ref=src, dst_ref=dst, send_sem=ss.at[number], recv_sem=rs.at[number],
            device_id=device, device_id_type=MESH,
        )

    sent = []

    def start(cp):
        cp.start()
        sent.append(cp)
        return cp

    load = pltpu.make_async_copy(grads_hbm, grads, local_sem.at[0])
    load.start()

    me_diag = dp == z * 2 + h
    barrier = pltpu.get_barrier_semaphore()
    greet = [at(dc=1), at(dh=1), at(1), at(-1), at(2), at(-2)]
    greet += [dp_at(dx, dy) for dx in range(2) for dy in range(8) if (dx, dy) != (0, 0)]
    for device in greet:
        pl.semaphore_signal(barrier, inc=1, device_id=device, device_id_type=MESH)
    for q in range(2):
        @pl.when(jnp.logical_not(jnp.logical_and(me_diag, h == q)))
        def _():
            pl.semaphore_signal(barrier, inc=1, device_id=(z * 2 + q, dp * 2 + c), device_id_type=MESH)

    mine = basis[:, pl.ds(pl.multiple_of(c * HALF, HALF), HALF)].T
    theirs = basis[:, pl.ds(pl.multiple_of((1 - c) * HALF, HALF), HALF)].T
    order = [4, 3, 5, 2, 6, 1, 7, 0]
    cores = {}
    for n, k in enumerate(order):
        tok = pl.ds(pl.multiple_of(((z + k) % 8) * TOK, TOK), TOK)
        chunk = acts[:, tok]
        csend[k] = jnp.dot(theirs, chunk, preferred_element_type=F32).astype(BF16)
        own[k] = jnp.dot(mine, chunk, preferred_element_type=F32)
        if n == 0:
            pl.semaphore_wait(barrier, 23 - jnp.where(me_diag, 1, 0))
        cores[k] = start(copy(csend.at[k], crecv.at[k], CORE + k, at(dc=1)))

    def rows_of(direction, stream):
        half = direction ^ stream
        return slice(half * Q, half * Q + Q)

    def slot(direction, stream, hop):
        return direction * 7 + stream * 4 + hop

    def added(k, rows):
        return own[k, rows, :] + crecv[k, rows, :].astype(F32)

    ring = {}

    def ring_send(direction, stream, hop):
        left = (4 - hop) if stream == 0 else (3 - hop)
        k = (8 - left) % 8 if direction == 0 else left
        n = slot(direction, stream, hop)
        value = added(k, rows_of(direction, stream))
        if hop:
            value = value + rrecv[slot(direction, stream, hop - 1)].astype(F32)
        rsend[n] = value.astype(BF16)
        ring[n] = start(copy(rsend.at[n], rrecv.at[n], RING + n, at(-1 if direction == 0 else 1)))

    cores[4].wait_recv()
    ring_send(0, 0, 0)
    ring_send(1, 0, 0)
    cores[5].wait_recv()
    ring_send(0, 1, 0)
    cores[3].wait_recv()
    ring_send(1, 1, 0)
    for k in order[3:]:
        cores[k].wait_recv()
    for hop in range(1, 4):
        for stream in range(2):
            if stream == 1 and hop == 3:
                continue
            for direction in range(2):
                ring[slot(direction, stream, hop - 1)].wait_recv()
                ring_send(direction, stream, hop)

    pairs = []
    for half in (1, 0):
        rows = slice(half * Q, half * Q + Q)
        total = added(0, rows)
        for direction in range(2):
            stream = direction ^ half
            n = slot(direction, stream, 3 if stream == 0 else 2)
            ring[n].wait_recv()
            total = total + rrecv[n].astype(F32)
        xsend[half] = total.astype(BF16)
        pairs.append(start(copy(xsend.at[half], xrecv.at[half], XHI + half, at(dh=1))))

    def piece(k, half):
        return proj.at[(z + k + 8) % 8, pl.ds(pl.multiple_of(c * HALF + half * Q, Q), Q)]

    gath, shared = {}, {}

    def gath_send(direction, stream, hop):
        half = direction ^ stream
        k = hop if direction == 0 else -hop
        n = slot(direction, stream, hop)
        ref = piece(k, half)
        gath[n] = start(copy(ref, ref, GATH + n, at(-1 if direction == 0 else 1)))

    def share(k, half):
        ref = piece(k, half)
        n = (k % 8) * 2 + half
        shared[n] = start(copy(ref, ref, SHARE + n, at(dc=1)))

    def multiply(k):
        zk = (z + k + 8) % 8
        for half in range(2):
            shared[(k % 8) * 2 + half].wait_recv()
        part = jnp.dot(
            proj[zk], grads[pl.ds(pl.multiple_of(zk * TOK, TOK), TOK), :], preferred_element_type=F32
        )
        if k == 0:
            acc[...] = part
        else:
            acc[...] += part

    for cp, half in zip(pairs, (1, 0)):
        cp.wait_recv()
        total = xsend[half].astype(F32) + xrecv[half].astype(F32)
        proj[z, pl.ds(pl.multiple_of(c * HALF + half * Q, Q), Q), :] = total.astype(BF16)
        gath_send(half, 0, 0)
        gath_send(1 - half, 1, 0)
        share(0, half)
    load.wait()
    multiply(0)
    for hop in range(1, 5):
        for stream in range(2):
            if stream == 1 and hop == 4:
                continue
            for direction in range(2):
                half = direction ^ stream
                gath[slot(direction, stream, hop - 1)].wait_recv()
                if hop < (4 if stream == 0 else 3):
                    gath_send(direction, stream, hop)
                share(hop if direction == 0 else -hop, half)
        if hop > 1:
            multiply(hop - 1)
            multiply(1 - hop)
    multiply(4)

    low[...] = acc[...].astype(BF16)
    dps = []
    for dx, dy in sorted(
        [(dx, dy) for dx in range(2) for dy in range(8) if (dx, dy) != (0, 0)],
        key=lambda o: (-min(o[1], 8 - o[1]), -o[0]),
    ):
        n = dx * 8 + dy
        device = dp_at(dx, dy)
        rows = pl.ds(pl.multiple_of(device[0] * ROWS, ROWS), ROWS)
        dps.append((n, start(copy(low.at[rows], lowr.at[n], DPX + n, device))))
    total = low[pl.ds(pl.multiple_of(dp * ROWS, ROWS), ROWS), :].astype(F32)
    for n, cp in reversed(dps):
        cp.wait_recv()
        total = total + lowr[n].astype(F32)

    m = 0.9 * moment[...] + 0.1 * total
    v = 0.95 * second[...] + 0.05 * total * total
    moment_new[...] = m
    second_new[...] = v
    step[...] = (m / (jnp.sqrt(v) + 1e-8)).astype(BF16)

    def target(q):
        return (z * 2 + q, dp * 2 + c)

    rows = pl.ds(pl.multiple_of(dp * ROWS, ROWS), ROWS)
    group = z * 2 + h
    for q in range(2):
        here = jnp.logical_and(me_diag, h == q)

        @pl.when(here)
        def _():
            steps[c, rows, :] = step[...]

        @pl.when(jnp.logical_not(here))
        def _():
            pltpu.make_async_remote_copy(
                src_ref=step, dst_ref=steps.at[c, rows], send_sem=ss.at[TRAN + q],
                recv_sem=rs.at[TRAN + dp % 2],
                device_id=(group, (dp // 2) * 4 + q * 2 + c), device_id_type=MESH,
            ).start()
    for q in range(2):
        @pl.when(jnp.logical_not(jnp.logical_and(me_diag, h == q)))
        def _():
            pltpu.make_async_remote_copy(
                src_ref=step, dst_ref=steps.at[c, rows], send_sem=ss.at[TRAN + q],
                recv_sem=rs.at[TRAN + q],
                device_id=(group, (dp // 2) * 4 + q * 2 + c), device_id_type=MESH,
            ).wait()

    def srows(k, half=None):
        zk = (z + k + 8) % 8
        if half is None:
            return steps.at[c, pl.ds(pl.multiple_of(zk * 64, 64), 64)]
        return steps.at[c, pl.ds(pl.multiple_of(zk * 64 + half * ROWS, ROWS), ROWS)]

    def pass_on(number, k, dz, half=None):
        ref = srows(k, half)
        return start(copy(ref, ref, STEP + number, at(dz)))

    handed = []

    def hand(number, k, half=None):
        ref = srows(k, half)
        handed.append(start(copy(ref, ref, SHST + number, at(dc=1))))

    far = [pass_on(0, 0, -2), pass_on(1, 0, 2)]
    near = [pass_on(2, 0, -1), pass_on(3, 0, 1)]
    hand(0, 0)
    far[0].wait_recv()
    relay = [pass_on(4, 2, -2, 0), pass_on(6, 2, -1)]
    hand(1, 2)
    far[1].wait_recv()
    relay += [pass_on(5, -2, 2, 1), pass_on(7, -2, 1)]
    hand(2, -2)
    near[0].wait_recv()
    hand(3, 1)
    near[1].wait_recv()
    hand(4, -1)
    relay[1].wait_recv()
    hand(5, 3)
    relay[3].wait_recv()
    hand(6, -3)
    relay[0].wait_recv()
    hand(7, 4, 0)
    relay[2].wait_recv()
    hand(8, -4, 1)
    for cp in handed:
        cp.wait_recv()

    whole = basis[...]
    dense[:, :COLS] = jnp.dot(whole, steps[0], preferred_element_type=F32).astype(BF16)
    dense[:, COLS:] = jnp.dot(whole, steps[1], preferred_element_type=F32).astype(BF16)
    for cp in sent:
        cp.wait_send()


def shards(acts, grads, basis, moment, second):
    vmem = pl.BlockSpec(memory_space=pltpu.VMEM)
    return pl.pallas_call(
        kernel,
        out_shape=(
            jax.ShapeDtypeStruct(moment.shape, F32),
            jax.ShapeDtypeStruct(second.shape, F32),
            jax.ShapeDtypeStruct((256, 896), BF16),
        ),
        in_specs=[vmem, vmem, pl.BlockSpec(memory_space=pl.ANY), vmem, vmem],
        out_specs=(vmem, vmem, vmem),
        scratch_shapes=[
            pltpu.VMEM((2048, COLS), BF16),
            pltpu.VMEM((8, HALF, TOK), F32),
            pltpu.VMEM((8, HALF, TOK), BF16),
            pltpu.VMEM((8, HALF, TOK), BF16),
            pltpu.VMEM((14, Q, TOK), BF16),
            pltpu.VMEM((14, Q, TOK), BF16),
            pltpu.VMEM((2, Q, TOK), BF16),
            pltpu.VMEM((2, Q, TOK), BF16),
            pltpu.VMEM((8, 512, TOK), BF16),
            pltpu.VMEM((512, COLS), F32),
            pltpu.VMEM((512, COLS), BF16),
            pltpu.VMEM((16, ROWS, COLS), BF16),
            pltpu.VMEM((ROWS, COLS), BF16),
            pltpu.VMEM((2, 512, COLS), BF16),
            pltpu.SemaphoreType.DMA((1,)),
            pltpu.SemaphoreType.DMA((COUNT,)),
            pltpu.SemaphoreType.DMA((COUNT,)),
        ],
        compiler_params=pltpu.CompilerParams(
            collective_id=0, has_side_effects=True, vmem_limit_bytes=48 * 2**20
        ),
    )(acts, basis, grads, moment, second)


def solution(mesh):
    in_specs = (P("fsdp", "dp"), P("dp", "fsdp"), P("fsdp", None), P("dp", "fsdp"), P("dp", "fsdp"))
    out_specs = (P("dp", "fsdp"), P("dp", "fsdp"), P("fsdp", "dp"))
    return jax.shard_map(shards, mesh=mesh, in_specs=in_specs, out_specs=out_specs, check_vma=False)
```

time: 458 us -> 98.2 us (0.21); the launches traced: 451 us -> 96.8 us
  waiting for transfers between devices: 344 us -> 0 us
  Pallas kernels: 0 us -> 91.2 us
  blocking collectives: 78.5 us -> 0 us
  between operations: 14.1 us -> 0.71 us
  matrix products: 7.56 us -> 0 us
    psum x1 -> x0, waiting for transfers between devices: 280 us -> none  [shards(): whole_proj = lax.psum(partial_proj.astype(jnp.bfloat16), 'fsdp')]
    pallas_call x0 -> x1, Pallas kernels: none -> 91.2 us  [shards(): pl.pallas_call(kernel, out_shape=(jax.ShapeDtypeStruct(moment.shape, F32)...]
    reduce_scatter x1 -> x0, waiting for transfers between devices: 63.8 us -> none  [shards(): lax.psum_scatter(low_partial.astype(jnp.bfloat16), 'dp', scatter_dimensio...]
    all_gather x1 -> x0, blocking collectives: 53.6 us -> none  [shards(): all_columns = lax.all_gather(step_dir, 'fsdp', axis=1, tiled=True)]
    all_to_all x1 -> x0, blocking collectives: 24.9 us -> none  [shards(): lax.all_to_all(all_columns, 'dp', split_axis=1, concat_axis=0, tiled=True)]
    dot_general x3 -> x0, matrix products: 7.56 us -> none  [the longest x1 3.68 us: shards(): lax.dot_general(whole_proj, grads, (((0,), (0,)), ((), ())), preferred_el...]
  transfers between devices with their start and end apart: 2 -> 0, of which waited for: 2 -> 0; matrix products, arithmetic and copies ran while one was open for 0% -> 0% of each run, Pallas kernels for 0% -> 0%
where the time goes in v1:
time: 98.2 us; the launch traced here: 96.8 us
  Pallas kernels  91.2 us (93%)
  local copies, waits for them, and re-layouts  4.96 us (5%)
    pallas_call x1, Pallas kernels, shards(): pl.pallas_call(kernel, out_shape=(jax.ShapeDtypeStruct(moment.shape, F32)...  91.2 us
    unnamed x12, local copies, waits for them, and re-layouts  4.96 us

profile of v1, /device:TPU:7, one launch (start us, length us, event | category | flops | bytes accessed | tf_op | source)
XLA Modules:
  0.0 96.8 jit_solution(12007431942648202869)
XLA Ops:
  0.6 0.0 copy-start.3
  0.6 0.0 copy-start.2
  0.7 0.0 copy-start.1
  0.7 0.0 copy-start
  0.7 2.9 %copy.8.grads_hbm = bf16[2048,448]{1,0:T(8,128)(2,1)S(1)} copy(bf16[2048,448]{0,1:T(8,128)(2,1)} %param.6) | data formatting | bytes 3670016 | tf_op args[1]
  3.6 0.0 copy-done.3
  3.6 0.0 copy-done.2
  3.6 0.0 copy-done.1
  3.6 0.0 copy-done
  3.6 91.2 %shard_map.76 = (f32[32,448]{1,0:T(8,128)S(1)}, f32[32,448]{1,0:T(8,128)S(1)}, bf16[256,896]{1,0:T(8,128)(2,1)S(1)}) custom-call(bf16[256,2048]{1,0:T(8,128)(2,1)S(1)} %copy-done, bf16[256,512]{1,0:T(8,128)(2,1)S(1)} %copy-done.1, bf16[2048,448]{1,0:T(8,128)(2,1)S(1)} %copy.8.grads_hbm, f32[32,448]{1,0:T(8,128)S(1)} %copy-done.2, f32[32,448]{1,0:T(8,128)S(1)} %copy-done.3), custom_call_target="tpu_custom_call" | custom-call | tf_op jit(solution)/shard_map/pallas_call | solution.py:287
  94.8 0.6 copy.12
  95.4 0.6 copy.13
  96.1 0.8 copy.14
Async XLA Ops:
  0.6 3.0 %copy-start.3 = (f32[32,448]{1,0:T(8,128)S(1)}, f32[32,448]{1,0:T(8,128)}, u32[]{:S(2)}) copy-start(f32[32,448]{1,0:T(8,128)} %second.1) | copy-start | bytes 172036
  0.6 3.0 %copy-start.2 = (f32[32,448]{1,0:T(8,128)S(1)}, f32[32,448]{1,0:T(8,128)}, u32[]{:S(2)}) copy-start(f32[32,448]{1,0:T(8,128)} %moment.1) | copy-start | bytes 172036
  0.7 3.0 %copy-start.1 = (bf16[256,512]{1,0:T(8,128)(2,1)S(1)}, bf16[256,512]{1,0:T(8,128)(2,1)}, u32[]{:S(2)}) copy-start(bf16[256,512]{1,0:T(8,128)(2,1)} %basis.1) | copy-start | bytes 786436
  0.7 3.0 %copy-start = (bf16[256,2048]{1,0:T(8,128)(2,1)S(1)}, bf16[256,2048]{1,0:T(8,128)(2,1)}, u32[]{:S(2)}) copy-start(bf16[256,2048]{1,0:T(8,128)(2,1)} %acts.1) | copy-start | bytes 3145732

commit v2 on v0

v2 whole, which is shorter than its diff:
```python
import heapq

import jax
import jax.numpy as jnp
from jax import lax
from jax.experimental import pallas as pl
from jax.experimental.pallas import tpu as pltpu
from jax.sharding import PartitionSpec as P

F32 = jnp.float32
BF16 = jnp.bfloat16
MESH = pl.DeviceIdType.MESH
TOK = 256
KEPT = 128
Q = 64
COLS = 448
R = 16
ORDER = (4, 3, 5, 2, 6, 1, 7, 0)

CORE = 0
RING = 2
XHI = 16
GATH = 18
SHARE = 32
DPX = 40
TRAN = 56
STEP = 58
SHST = 66
RELAY = 75
COUNT = 83


class Message:
    def __init__(self, copy, arrival):
        self.copy, self.arrival = copy, arrival


class Plan:
    def __init__(self):
        self.now, self.heap, self.count, self.free = 0.0, [], 0, {}
        self.sent = []

    def spend(self, cost):
        self.now += cost

    def arrive(self, copy, path, kib):
        message = Message(copy, self.arrival(path, kib))
        self.sent.append(message)
        return message

    def arrival(self, path, kib):
        if path is None:
            return self.now + 0.85 + kib / 1000
        each = kib * 0.0227
        start = max([self.now] + [self.free.get(link, 0.0) for link, _ in path])
        for link, hops in path:
            self.free[link] = max(self.free.get(link, 0.0), self.now) + each * hops
        self.spend(0.03)
        return start + each + 1.95 + 0.6 * sum(hops for _, hops in path)

    def when(self, messages, action, ready=0.0):
        ready = max([ready] + [m.arrival for m in messages])
        heapq.heappush(self.heap, (ready, self.count, messages, action))
        self.count += 1

    def run(self):
        while self.heap:
            ready, _, messages, action = heapq.heappop(self.heap)
            while self.sent and self.sent[0].arrival < self.now - 1 and self.now + 0.2 < ready:
                self.sent.pop(0).copy.wait_send()
                self.spend(0.05)
            self.now = max(self.now, ready)
            for m in messages:
                m.copy.wait_recv()
            action()


def kernel(
    acts_hbm, basis_hbm, grads_hbm, moment_hbm, second_hbm,
    moment_new, second_new, dense,
    acts, basis, grads, moment, second,
    lhs, feats, own, csend, crecv, rsend, rrecv, xsend, xrecv, psend, precv, pown, fsend, frecv, proj, acc, low, lowr, step, steps, wide,
    local_sem, ss, rs,
):
    dp, fs = lax.axis_index("dp"), lax.axis_index("fsdp")
    xl, y = dp // 8, dp % 8
    z, h, c = fs // 4, (fs // 2) % 2, fs % 2

    def at(dz=0, dh=0, dc=0):
        return (dp, ((z + dz + 8) % 8) * 4 + ((h + dh) % 2) * 2 + (c + dc) % 2)

    def dp_at(dx, dy):
        return (((xl + dx) % 2) * 8 + (y + dy) % 8, fs)

    plan = Plan()

    def send(s, src, dst, number, device, path, kib):
        cp = pltpu.make_async_remote_copy(
            src_ref=src, dst_ref=dst, send_sem=ss.at[s * COUNT + number], recv_sem=rs.at[s * COUNT + number],
            device_id=device, device_id_type=MESH,
        )
        cp.start()
        return plan.arrive(cp, path, kib)

    diagonal = jnp.logical_and(dp == z * 2 + h, y == z)
    barrier = pltpu.get_barrier_semaphore()
    greet = [at(dc=1), at(dh=1), at(1), at(-1), at(2), at(-2)]
    greet += [dp_at(dx, dy) for dx in range(2) for dy in range(8) if (dx, dy) != (0, 0)]
    for device in greet:
        pl.semaphore_signal(barrier, inc=1, device_id=device, device_id_type=MESH)
    loads = []
    for n, (src, dst) in enumerate((
        (basis_hbm, basis), (acts_hbm, acts), (grads_hbm, grads), (moment_hbm, moment), (second_hbm, second),
    )):
        loads.append(pltpu.make_async_copy(src, dst, local_sem.at[n]))
        loads[-1].start()

    loads[0].wait()
    for j in range(4):
        block = basis[:, j * 128 : j * 128 + 128].T
        place = jnp.where(c == j // 2, 1, 0)
        for b in range(4):
            for s in range(2):
                row = ((j % 2) * 4 + b) * R
                lhs[s, place, row : row + R] = block[b * 32 + s * R : b * 32 + s * R + R]
    loads[1].wait()

    def rows_of(half):
        return slice(half * Q, half * Q + Q)

    def slot(direction, half, hop):
        return direction * 7 + (0 if hop == 0 else 1 + (hop - 1) * 2 + half)

    def zlink(direction):
        return "z-" if direction == 0 else "z+"

    def partial(s, n):
        k = ORDER[n]
        tok = pl.ds(pl.multiple_of(((z + k) % 8) * TOK, TOK), TOK)
        both = jnp.dot(lhs[s].reshape(2 * KEPT, 256), acts[:, tok], preferred_element_type=F32)
        csend[s, n] = both[:KEPT].astype(BF16)
        own[s, n] = both[KEPT:]
        plan.spend(0.15)

    def exchange(s, part):
        first, last = ((0, 3), (3, 8))[part]
        for n in range(first, last):
            partial(s, n)
        if s == 1 and part == 0:
            pl.semaphore_wait(barrier, 21)
        place = pl.ds(first, last - first)
        m = send(s, csend.at[s, place], crecv.at[s, place], CORE + part, at(dc=1), None, 64 * (last - first))
        plan.when([m], lambda: ((pair_first, pair_rest), (reduce_start, reduce_rest))[s][part](s))

    def added(s, k, half):
        n = ORDER.index(k % 8)
        return own[s, n, rows_of(half), :] + crecv[s, n, rows_of(half), :].astype(F32)

    waiting = {}

    def ring_send(s, direction, half, hop, value):
        n = slot(direction, half, hop)
        rsend[s, n] = value.astype(BF16)
        plan.spend(0.08)
        hops = 2 if hop == 0 else 1
        sign = -1 if direction == 0 else 1
        m = send(s, rsend.at[s, n], rrecv.at[s, n], RING + n, at(sign * hops), [(zlink(direction), hops)], 32)
        if hop == 0:
            waiting[s, direction, half] = m
        else:
            plan.when([m], lambda: ring_next(s, direction, half, hop))

    def reduce_start(s):
        for direction in range(2):
            ring_send(s, direction, direction, 0, added(s, 4, direction))
        for half in range(2):
            for direction in range(2):
                k = 5 if direction == 0 else 3
                ring_send(s, direction, half ^ direction ^ 1, 1, added(s, k, half ^ direction ^ 1))

    ready = {0: False, 1: False}
    held = {0: [], 1: []}

    def reduce_rest(s):
        ready[s] = True
        for action in held[s]:
            action()

    sums = {}

    def ring_next(s, direction, half, hop):
        if not ready[s]:
            held[s].append(lambda: ring_next(s, direction, half, hop))
            return
        arrived = rrecv[s, slot(direction, half, hop)].astype(F32)
        if hop == 1 and half == direction:
            m = waiting[s, direction, half]
            m.copy.wait_recv()
            plan.now = max(plan.now, m.arrival)
            arrived = arrived + rrecv[s, slot(direction, half, 0)].astype(F32)
        if hop < 3:
            k = hop - 3 if direction == 0 else 3 - hop
            ring_send(s, direction, half, hop + 1, added(s, k, half) + arrived)
            return
        sums.setdefault((s, half), []).append(direction)
        if len(sums[s, half]) == 2:
            total = added(s, 0, half)
            for d in range(2):
                total = total + rrecv[s, slot(d, half, 3)].astype(F32)
            xsend[s, half] = total.astype(BF16)
            plan.spend(0.1)
            m = send(s, xsend.at[s, half], xrecv.at[s, half], XHI + half, at(dh=1), [("x", 1), ("x2", 1)], 32)
            plan.when([m], lambda: gather_start(s, half))

    mine = pl.multiple_of(h * Q, Q)
    theirs = pl.multiple_of((1 - h) * Q, Q)

    def pair(s, part):
        first, last = ((0, 3), (3, 8))[part]
        for n in range(first, last):
            for rows, out in ((theirs, None), (mine, own)):
                rows = pl.ds(rows, Q)
                value = own[s, n, rows, :] + crecv[s, n, rows, :].astype(F32)
                if out is None:
                    psend[n] = value.astype(BF16)
                else:
                    pown[n] = value
            plan.spend(0.1)
        place = pl.ds(first, last - first)
        m = send(
            s, psend.at[place], precv.at[place], XHI + part, at(dh=1), [("x", 1), ("x2", 1)], 32 * (last - first)
        )
        plan.when([m], lambda: (paired_first, paired_rest)[part](s))

    def pair_first(s):
        pair(s, 0)

    def pair_rest(s):
        pair(s, 1)

    def paired(k):
        n = ORDER.index(k % 8)
        return pown[n] + precv[n].astype(F32)

    def pair_send(s, n, direction, hops, value, action):
        rows = slice(0, value.shape[0])
        fsend[n, rows, :] = value.astype(BF16)
        plan.spend(0.05)
        sign = -1 if direction == 0 else 1
        m = send(
            s, fsend.at[n, rows], frecv.at[n, rows], RING + n, at(sign * hops), [(zlink(direction), hops)],
            value.shape[0] // 2,
        )
        plan.when([m], action)

    need = {}

    def counted(key, limit, action):
        need[key] = need.get(key, 0) + 1
        if need[key] == limit:
            action()

    def paired_first(s):
        for direction in range(2):
            value = paired(4)[direction * 32 : direction * 32 + 32]
            pair_send(s, direction * 4, direction, 2, value, lambda d=direction: pair_collect(s, d))
        for direction in range(2):
            value = paired(-3 if direction == 0 else 3)
            pair_send(s, direction * 4 + 1, direction, 1, value, lambda d=direction: pair_collect(s, d))

    def paired_rest(s):
        for direction in range(2):
            value = paired(-1 if direction == 0 else 1)
            pair_send(s, direction * 4 + 2, direction, 1, value, lambda: pair_total(s))
        for direction in range(2):
            pair_collect(s, direction)

    def pair_collect(s, direction):
        def collected():
            n = direction * 4
            value = paired(-2 if direction == 0 else 2) + frecv[n + 1].astype(F32)
            half = frecv[n, 0:32, :].astype(F32)
            zero = jnp.zeros_like(half)
            value = value + jnp.concatenate([half, zero] if direction == 0 else [zero, half], axis=0)
            pair_send(s, n + 3, direction, 2, value, lambda: pair_total(s))

        counted(("collect", direction), 3, collected)

    def pair_total(s):
        def totalled():
            value = paired(0)
            for n in (2, 3, 6, 7):
                value = value + frecv[n].astype(F32)
            proj[s, z, pl.ds(pl.multiple_of(c * KEPT + h * Q, Q), Q), :] = value.astype(BF16)
            plan.spend(0.1)
            pair_gather(s)

        counted("total", 4, totalled)

    def fpiece(s, k, half=None):
        row = c * KEPT + h * Q + (0 if half is None else half * 32)
        rows = pl.ds(pl.multiple_of(row, 32), Q if half is None else 32)
        return proj.at[s, (z + k + 8) % 8, rows]

    def pair_gather(s):
        def relay(k):
            ref = fpiece(s, k)
            m = send(s, ref, ref, RELAY + k % 8, at(dh=1), [("x", 1), ("x2", 1)], 32)
            plan.when([m], lambda: arrived_piece(s, k))
            arrived_piece(s, k)

        def pass_on(number, k, dz, action, half=None):
            ref = fpiece(s, k, half)
            link = zlink(0 if dz < 0 else 1)
            m = send(s, ref, ref, GATH + number, at(dz), [(link, abs(dz))], 32 if half is None else 16)
            plan.when([m], action)

        def farthest():
            counted("farthest", 2, lambda: relay(4))

        def from_above():
            pass_on(4, 2, -2, farthest, 0)
            pass_on(6, 2, -1, lambda: relay(3))
            relay(2)

        def from_below():
            pass_on(5, -2, 2, farthest, 1)
            pass_on(7, -2, 1, lambda: relay(-3))
            relay(-2)

        pass_on(0, 0, -2, from_above)
        pass_on(1, 0, 2, from_below)
        pass_on(2, 0, -1, lambda: relay(1))
        pass_on(3, 0, 1, lambda: relay(-1))
        relay(0)

    def piece(s, k, half):
        return proj.at[s, (z + k + 8) % 8, pl.ds(pl.multiple_of(c * KEPT + half * Q, Q), Q)]

    def gath_send(s, direction, half, hop, k, hops=1):
        sign = -1 if direction == 0 else 1
        ref = piece(s, k, half)
        n = slot(direction, half, 3 - hop) if hops == 1 else slot(direction, half, 0)
        m = send(s, ref, ref, GATH + n, at(sign * hops), [(zlink(direction), hops)], 32)
        plan.when([m], lambda: gathered(s, direction, half, hop + hops))

    have = {}

    def arrived_piece(s, k):
        have[s, k] = have.get((s, k), 0) + 1
        if have[s, k] == 2:
            ref = proj.at[s, (z + k + 8) % 8, pl.ds(pl.multiple_of(c * KEPT, KEPT), KEPT)]
            m = send(s, ref, ref, SHARE + k % 8, at(dc=1), None, 64)
            plan.when([m], lambda: multiply(s, k))

    def gather_start(s, half):
        total = xsend[s, half].astype(F32) + xrecv[s, half].astype(F32)
        proj[s, z, pl.ds(pl.multiple_of(c * KEPT + half * Q, Q), Q), :] = total.astype(BF16)
        plan.spend(0.1)
        for direction in range(2):
            gath_send(s, direction, half, 0, 0)
        arrived_piece(s, 0)

    def gathered(s, direction, half, hop):
        sign = 1 if direction == 0 else -1
        if hop == 2 and half == direction:
            gath_send(s, direction, half, 2, sign * 2, hops=2)
        if hop < 3:
            gath_send(s, direction, half, hop, sign * hop)
        arrived_piece(s, sign * hop if hop < 4 else 4)

    loaded = []
    done = {0: 0, 1: 0}

    def multiply(s, k):
        if not loaded:
            loads[2].wait()
            loaded.append(True)
        zk = (z + k + 8) % 8
        part = lax.dot_general(
            proj[s, zk], grads[:, pl.ds(pl.multiple_of(zk * TOK, TOK), TOK)],
            (((1,), (1,)), ((), ())), preferred_element_type=F32,
        )
        plan.spend(0.3)
        done[s] += 1
        if done[s] == 1:
            acc[s] = part
        elif done[s] < 8:
            acc[s] += part
        else:
            low[s] = (acc[s] + part).astype(BF16)
            over_dp(s)

    def over_dp(s):
        messages = []
        offsets = [(dx, dy) for dx in range(2) for dy in range(8) if (dx, dy) != (0, 0)]
        for dx, dy in sorted(offsets, key=lambda o: (-min(o[1], 8 - o[1]), -o[0])):
            n = dx * 8 + dy
            device = dp_at(dx, dy)
            path = [("y+", dy)] if dy < 4 else [("y-", 8 - dy)] if dy > 4 else [("y+", 2), ("y-", 2)]
            rows = pl.ds(pl.multiple_of(device[0] * R, R), R)
            messages.append((n, send(s, low.at[s, rows], lowr.at[s, n], DPX + n, device, path, 16)))
        plan.when([m for _, m in messages], lambda: adam(s, [n for n, _ in messages]))

    def adam(s, numbers):
        if "adam" not in need:
            need["adam"] = 1
            loads[3].wait()
            loads[4].wait()
        total = low[s, pl.ds(pl.multiple_of(dp * R, R), R), :].astype(F32)
        for n in numbers:
            total = total + lowr[s, n].astype(F32)
        rows = slice(s * R, s * R + R)
        m = 0.9 * moment[rows] + 0.1 * total
        v = 0.95 * second[rows] + 0.05 * total * total
        moment_new[rows] = m
        second_new[rows] = v
        step[s] = (m / (jnp.sqrt(v) + 1e-8)).astype(BF16)
        plan.spend(0.3)

        place = pl.ds(pl.multiple_of(y * R, R), R)
        for q in range(2):
            here = jnp.logical_and(diagonal, h == q)

            @pl.when(here)
            def _():
                steps[c, s, xl, place, :] = step[s]

            @pl.when(jnp.logical_not(here))
            def _():
                turn(s, q, xl).start()
        plan.when([], lambda: turned(s), ready=plan.now + 6)

    def turn(s, q, origin):
        place = pl.ds(pl.multiple_of(y * R, R), R)
        return pltpu.make_async_remote_copy(
            src_ref=step.at[s], dst_ref=steps.at[c, s, xl, place], send_sem=ss.at[s * COUNT + TRAN + q],
            recv_sem=rs.at[s * COUNT + TRAN + origin],
            device_id=(z * 2 + h, y * 4 + q * 2 + c), device_id_type=MESH,
        )

    def turned(s):
        for q in range(2):
            @pl.when(jnp.logical_not(jnp.logical_and(diagonal, xl == q)))
            def _():
                turn(s, q, q).wait_recv()
        spread(s)

    def srows(s, k, half=None):
        place = pl.ds(pl.multiple_of(((z + k + 8) % 8) * R, R), R)
        if half is None:
            return steps.at[c, s, :, place]
        return steps.at[c, s, half, place]

    def spread(s):
        def hand(number, k, half=None):
            ref = srows(s, k, half)
            m = send(s, ref, ref, SHST + number, at(dc=1), None, 32)
            plan.when([m], lambda: counted(("other", s), 9, lambda: finished(s, "other")))
            if number:
                counted(("this", s), 8, lambda: finished(s, "this"))

        def pass_on(number, k, dz, action, half=None):
            ref = srows(s, k, half)
            link = zlink(0 if dz < 0 else 1)
            m = send(s, ref, ref, STEP + number, at(dz), [(link, abs(dz))], 32 if half is None else 16)
            plan.when([m], action)

        def from_above():
            pass_on(4, 2, -2, lambda: hand(7, 4, 0), 0)
            pass_on(6, 2, -1, lambda: hand(5, 3))
            hand(1, 2)

        def from_below():
            pass_on(5, -2, 2, lambda: hand(8, 4, 1), 1)
            pass_on(7, -2, 1, lambda: hand(6, -3))
            hand(2, -2)

        pass_on(0, 0, -2, from_above)
        pass_on(1, 0, 2, from_below)
        pass_on(2, 0, -1, lambda: hand(3, 1))
        pass_on(3, 0, 1, lambda: hand(4, -1))
        hand(0, 0)

    def natural():
        for s in range(2):
            both = [lhs[s, jnp.where(c == core, 1, 0)] for core in range(2)]
            feats[s] = jnp.concatenate(both, axis=0).T

    ends = []

    def finished(s, which):
        columns = c if which == "this" else 1 - c
        value = jnp.dot(feats[s], steps[columns, s].reshape(256, COLS), preferred_element_type=F32)
        if which not in ends:
            wide[columns] = value
        else:
            wide[columns] += value
        plan.spend(0.2)
        ends.append(which)
        if len(ends) == 4:
            for half in range(2):
                dense[:, half * COLS : half * COLS + COLS] = wide[half].astype(BF16)

    exchange(1, 0)
    plan.when([], lambda: exchange(0, 0), ready=plan.now)
    plan.when([], lambda: exchange(1, 1), ready=plan.now + 0.01)
    plan.when([], lambda: exchange(0, 1), ready=plan.now + 0.02)
    plan.when([], natural, ready=plan.now + 5)
    plan.run()
    for m in plan.sent:
        m.copy.wait_send()
    for s in range(2):
        for q in range(2):
            @pl.when(jnp.logical_not(jnp.logical_and(diagonal, h == q)))
            def _():
                turn(s, q, 0).wait_send()


def store(a, b, c, a_out, b_out, c_out):
    a_out[...] = a[...]
    b_out[...] = b[...]
    c_out[...] = c[...]


def shards(acts, grads, basis, moment, second):
    vmem = pl.BlockSpec(memory_space=pltpu.VMEM)
    hbm = pl.BlockSpec(memory_space=pltpu.HBM)
    results = pl.pallas_call(
        kernel,
        out_shape=(
            jax.ShapeDtypeStruct(moment.shape, F32),
            jax.ShapeDtypeStruct(second.shape, F32),
            jax.ShapeDtypeStruct((256, 896), BF16),
        ),
        in_specs=[hbm] * 5,
        out_specs=(vmem, vmem, vmem),
        scratch_shapes=[
            pltpu.VMEM((256, 2048), BF16),
            pltpu.VMEM((256, 512), BF16),
            pltpu.VMEM((COLS, 2048), BF16),
            pltpu.VMEM((32, COLS), F32),
            pltpu.VMEM((32, COLS), F32),
            pltpu.VMEM((2, 2, KEPT, 256), BF16),
            pltpu.VMEM((2, 256, 256), BF16),
            pltpu.VMEM((2, 8, KEPT, TOK), F32),
            pltpu.VMEM((2, 8, KEPT, TOK), BF16),
            pltpu.VMEM((2, 8, KEPT, TOK), BF16),
            pltpu.VMEM((2, 14, Q, TOK), BF16),
            pltpu.VMEM((2, 14, Q, TOK), BF16),
            pltpu.VMEM((2, 2, Q, TOK), BF16),
            pltpu.VMEM((2, 2, Q, TOK), BF16),
            pltpu.VMEM((8, Q, TOK), BF16),
            pltpu.VMEM((8, Q, TOK), BF16),
            pltpu.VMEM((8, Q, TOK), F32),
            pltpu.VMEM((8, Q, TOK), BF16),
            pltpu.VMEM((8, Q, TOK), BF16),
            pltpu.VMEM((2, 8, 2 * KEPT, TOK), BF16),
            pltpu.VMEM((2, 2 * KEPT, COLS), F32),
            pltpu.VMEM((2, 2 * KEPT, COLS), BF16),
            pltpu.VMEM((2, 16, R, COLS), BF16),
            pltpu.VMEM((2, R, COLS), BF16),
            pltpu.VMEM((2, 2, 2, 128, COLS), BF16),
            pltpu.VMEM((2, 256, COLS), F32),
            pltpu.SemaphoreType.DMA((5,)),
            pltpu.SemaphoreType.DMA((2 * COUNT,)),
            pltpu.SemaphoreType.DMA((2 * COUNT,)),
        ],
        compiler_params=pltpu.CompilerParams(
            collective_id=0, has_side_effects=True, vmem_limit_bytes=60 * 2**20
        ),
    )(acts, basis, grads.T, moment, second)
    return pl.pallas_call(
        store,
        out_shape=tuple(jax.ShapeDtypeStruct(r.shape, r.dtype) for r in results),
        in_specs=[vmem] * 3,
        out_specs=(vmem,) * 3,
    )(*results)


def solution(mesh):
    in_specs = (P("fsdp", "dp"), P("dp", "fsdp"), P("fsdp", None), P("dp", "fsdp"), P("dp", "fsdp"))
    out_specs = (P("dp", "fsdp"), P("dp", "fsdp"), P("fsdp", "dp"))
    return jax.shard_map(shards, mesh=mesh, in_specs=in_specs, out_specs=out_specs, check_vma=False)
```

time: 458 us -> 84.8 us (0.19); the launches traced: 451 us -> 84 us
  waiting for transfers between devices: 344 us -> 0 us
  Pallas kernels: 0 us -> 83.4 us
  blocking collectives: 78.5 us -> 0 us
  between operations: 14.1 us -> 0.64 us
  matrix products: 7.56 us -> 0 us
  local copies, waits for them, and re-layouts: 5 us -> 0 us
    psum x1 -> x0, waiting for transfers between devices: 280 us -> none  [shards(): whole_proj = lax.psum(partial_proj.astype(jnp.bfloat16), 'fsdp')]
    pallas_call x0 -> x2, Pallas kernels: none -> 83.4 us  [the longest x1 81.5 us: shards(): pl.pallas_call(kernel, out_shape=(jax.ShapeDtypeStruct(moment.shape, F32)...]
    reduce_scatter x1 -> x0, waiting for transfers between devices: 63.8 us -> none  [shards(): lax.psum_scatter(low_partial.astype(jnp.bfloat16), 'dp', scatter_dimensio...]
    all_gather x1 -> x0, blocking collectives: 53.6 us -> none  [shards(): all_columns = lax.all_gather(step_dir, 'fsdp', axis=1, tiled=True)]
    all_to_all x1 -> x0, blocking collectives: 24.9 us -> none  [shards(): lax.all_to_all(all_columns, 'dp', split_axis=1, concat_axis=0, tiled=True)]
    dot_general x3 -> x0, matrix products: 7.56 us -> none  [the longest x1 3.68 us: shards(): lax.dot_general(whole_proj, grads, (((0,), (0,)), ((), ())), preferred_el...]
  transfers between devices with their start and end apart: 2 -> 0, of which waited for: 2 -> 0; matrix products, arithmetic and copies ran while one was open for 0% -> 0% of each run, Pallas kernels for 0% -> 0%
where the time goes in v2:
time: 84.8 us; the launch traced here: 84 us
  Pallas kernels  83.4 us (98%)
    pallas_call x1, Pallas kernels, shards(): pl.pallas_call(kernel, out_shape=(jax.ShapeDtypeStruct(moment.shape, F32)...  81.5 us
    pallas_call x1, Pallas kernels, shards(): pl.pallas_call(store, out_shape=tuple((jax.ShapeDtypeStruct(r.shape, r.dt...  1.91 us

profile of v2, /device:TPU:7, one launch (start us, length us, event | category | flops | bytes accessed | tf_op | source)
XLA Modules:
  0.0 84.0 jit_solution(7238415901428660198)
XLA Ops:
  0.6 81.5 %shard_map.76 = (f32[32,448]{1,0:T(8,128)}, f32[32,448]{1,0:T(8,128)}, bf16[256,896]{1,0:T(8,128)(2,1)}) custom-call(bf16[256,2048]{1,0:T(8,128)(2,1)} %acts_hbm.1, bf16[256,512]{1,0:T(8,128)(2,1)} %basis_hbm.1, bf16[448,2048]{1,0:T(8,128)(2,1)} %bitcast.1, f32[32,448]{1,0:T(8,128)} %moment_hbm.1, f32[32,448]{1,0:T(8,128)} %second_hbm.1), custom_call_target="tpu_custom_call" | custom-call | tf_op jit(solution)/shard_map/pallas_call | solution.py:529
  82.1 1.9 %shard_map.77 = (f32[32,448]{1,0:T(8,128)}, f32[32,448]{1,0:T(8,128)}, bf16[256,896]{1,0:T(8,128)(2,1)}) custom-call(f32[32,448]{1,0:T(8,128)} %get-tuple-element.6.a, f32[32,448]{1,0:T(8,128)} %get-tuple-element.7.b, bf16[256,896]{1,0:T(8,128)(2,1)} %get-tuple-element.8.c), custom_call_target="tpu_custom_call" | custom-call | tf_op jit(solution)/shard_map/pallas_call | solution.py:573

commit v3 on v2

--- a/solution.py
+++ b/solution.py
@@ -14,7 +14,9 @@
 KEPT = 128
 Q = 64
 COLS = 448
+WIDE = 512
 R = 16
+DP_PAIR = (True, True)
 ORDER = (4, 3, 5, 2, 6, 1, 7, 0)
 
 CORE = 0
@@ -79,7 +81,7 @@
     acts_hbm, basis_hbm, grads_hbm, moment_hbm, second_hbm,
     moment_new, second_new, dense,
     acts, basis, grads, moment, second,
-    lhs, feats, own, csend, crecv, rsend, rrecv, xsend, xrecv, psend, precv, pown, fsend, frecv, proj, acc, low, lowr, step, steps, wide,
+    lhs, feats, own, csend, crecv, rsend, rrecv, xsend, xrecv, psend, precv, pown, fsend, frecv, proj, acc, low, lowr, lowx, step, steps, wide,
     local_sem, ss, rs,
 ):
     dp, fs = lax.axis_index("dp"), lax.axis_index("fsdp")
@@ -102,19 +104,19 @@
         cp.start()
         return plan.arrive(cp, path, kib)
 
-    diagonal = jnp.logical_and(dp == z * 2 + h, y == z)
-    barrier = pltpu.get_barrier_semaphore()
-    greet = [at(dc=1), at(dh=1), at(1), at(-1), at(2), at(-2)]
-    greet += [dp_at(dx, dy) for dx in range(2) for dy in range(8) if (dx, dy) != (0, 0)]
-    for device in greet:
-        pl.semaphore_signal(barrier, inc=1, device_id=device, device_id_type=MESH)
     loads = []
     for n, (src, dst) in enumerate((
         (basis_hbm, basis), (acts_hbm, acts), (grads_hbm, grads), (moment_hbm, moment), (second_hbm, second),
     )):
         loads.append(pltpu.make_async_copy(src, dst, local_sem.at[n]))
-        loads[-1].start()
-
+    loads[0].start()
+    loads[1].start()
+
+    barrier = pltpu.get_barrier_semaphore()
+    greet = [at(dc=1), at(dh=1), at(1), at(-1), at(2), at(-2)]
+    greet += [dp_at(1, 0)] + [dp_at(0, dy) for dy in range(1, 8)]
+    for device in greet:
+        pl.semaphore_signal(barrier, inc=1, device_id=device, device_id_type=MESH)
     loads[0].wait()
     for j in range(4):
         block = basis[:, j * 128 : j * 128 + 128].T
@@ -147,7 +149,7 @@
         for n in range(first, last):
             partial(s, n)
         if s == 1 and part == 0:
-            pl.semaphore_wait(barrier, 21)
+            pl.semaphore_wait(barrier, 14)
         place = pl.ds(first, last - first)
         m = send(s, csend.at[s, place], crecv.at[s, place], CORE + part, at(dc=1), None, 64 * (last - first))
         plan.when([m], lambda: ((pair_first, pair_rest), (reduce_start, reduce_rest))[s][part](s))
@@ -388,66 +390,75 @@
         elif done[s] < 8:
             acc[s] += part
         else:
-            low[s] = (acc[s] + part).astype(BF16)
+            low[s, :, :COLS] = (acc[s] + part).astype(BF16)
             over_dp(s)
 
     def over_dp(s):
+        if DP_PAIR[s]:
+            for dy in ORDER:
+                rows = pl.ds(pl.multiple_of(((1 - xl) * 8 + (y + dy) % 8) * R, R), R)
+                m = send(s, low.at[s, rows], lowx.at[s, dy], DPX + dy, dp_at(1, 0), [("xlo", 1)], 16)
+                plan.when([m], lambda dy=dy: over_y(s, dy))
+            return
         messages = []
         offsets = [(dx, dy) for dx in range(2) for dy in range(8) if (dx, dy) != (0, 0)]
         for dx, dy in sorted(offsets, key=lambda o: (-min(o[1], 8 - o[1]), -o[0])):
             n = dx * 8 + dy
             device = dp_at(dx, dy)
-            path = [("y+", dy)] if dy < 4 else [("y-", 8 - dy)] if dy > 4 else [("y+", 2), ("y-", 2)]
             rows = pl.ds(pl.multiple_of(device[0] * R, R), R)
-            messages.append((n, send(s, low.at[s, rows], lowr.at[s, n], DPX + n, device, path, 16)))
+            messages.append((n, send(s, low.at[s, rows], lowr.at[s, n], DPX + n, device, ypath(dy), 16)))
         plan.when([m for _, m in messages], lambda: adam(s, [n for n, _ in messages]))
+
+    def ypath(dy):
+        return [("y+", dy)] if dy < 4 else [("y-", 8 - dy)] if dy > 4 else [("y+", 2), ("y-", 2)]
+
+    pairs = {0: [], 1: []}
+
+    def over_y(s, dy):
+        rows = pl.ds(pl.multiple_of((xl * 8 + (y + dy) % 8) * R, R), R)
+        low[s, rows, :] = (low[s, rows, :].astype(F32) + lowx[s, dy].astype(F32)).astype(BF16)
+        plan.spend(0.04)
+        if dy:
+            n = 8 + dy
+            pairs[s].append(send(s, low.at[s, rows], lowr.at[s, n], DPX + n, dp_at(0, dy), ypath(dy), 16))
+        else:
+            plan.when(pairs[s], lambda: adam(s, [8 + k for k in ORDER[:7]]))
 
     def adam(s, numbers):
         if "adam" not in need:
             need["adam"] = 1
             loads[3].wait()
             loads[4].wait()
-        total = low[s, pl.ds(pl.multiple_of(dp * R, R), R), :].astype(F32)
+        total = low[s, pl.ds(pl.multiple_of(dp * R, R), R), :COLS].astype(F32)
         for n in numbers:
-            total = total + lowr[s, n].astype(F32)
+            total = total + lowr[s, n, :, :COLS].astype(F32)
         rows = slice(s * R, s * R + R)
         m = 0.9 * moment[rows] + 0.1 * total
         v = 0.95 * second[rows] + 0.05 * total * total
         moment_new[rows] = m
         second_new[rows] = v
-        step[s] = (m / (jnp.sqrt(v) + 1e-8)).astype(BF16)
+        step[s, :, :COLS] = (m / (jnp.sqrt(v) + 1e-8)).astype(BF16)
         plan.spend(0.3)
 
-        place = pl.ds(pl.multiple_of(y * R, R), R)
         for q in range(2):
-            here = jnp.logical_and(diagonal, h == q)
-
-            @pl.when(here)
-            def _():
-                steps[c, s, xl, place, :] = step[s]
-
-            @pl.when(jnp.logical_not(here))
-            def _():
-                turn(s, q, xl).start()
-        plan.when([], lambda: turned(s), ready=plan.now + 6)
+            turn(s, q, xl).start()
+        plan.when([], lambda: turned(s), ready=plan.now + 5.5)
 
     def turn(s, q, origin):
         place = pl.ds(pl.multiple_of(y * R, R), R)
         return pltpu.make_async_remote_copy(
             src_ref=step.at[s], dst_ref=steps.at[c, s, xl, place], send_sem=ss.at[s * COUNT + TRAN + q],
             recv_sem=rs.at[s * COUNT + TRAN + origin],
-            device_id=(z * 2 + h, y * 4 + q * 2 + c), device_id_type=MESH,
+            device_id=(z * 2 + h, ((y - z - h + 12) % 8) * 4 + q * 2 + c), device_id_type=MESH,
         )
 
     def turned(s):
         for q in range(2):
-            @pl.when(jnp.logical_not(jnp.logical_and(diagonal, xl == q)))
-            def _():
-                turn(s, q, q).wait_recv()
+            turn(s, q, q).wait_recv()
         spread(s)
 
     def srows(s, k, half=None):
-        place = pl.ds(pl.multiple_of(((z + k + 8) % 8) * R, R), R)
+        place = pl.ds(pl.multiple_of(((z + k + dp // 2 + dp % 2 + 12) % 8) * R, R), R)
         if half is None:
             return steps.at[c, s, :, place]
         return steps.at[c, s, half, place]
@@ -483,6 +494,8 @@
         hand(0, 0)
 
     def natural():
+        low[:, :, 384:] = jnp.zeros((2, 2 * KEPT, 128), BF16)
+        step[:, :, 384:] = jnp.zeros((2, R, 128), BF16)
         for s in range(2):
             both = [lhs[s, jnp.where(c == core, 1, 0)] for core in range(2)]
             feats[s] = jnp.concatenate(both, axis=0).T
@@ -491,7 +504,7 @@
 
     def finished(s, which):
         columns = c if which == "this" else 1 - c
-        value = jnp.dot(feats[s], steps[columns, s].reshape(256, COLS), preferred_element_type=F32)
+        value = jnp.dot(feats[s], steps[columns, s].reshape(256, WIDE)[:, :COLS], preferred_element_type=F32)
         if which not in ends:
             wide[columns] = value
         else:
@@ -507,20 +520,25 @@
     plan.when([], lambda: exchange(1, 1), ready=plan.now + 0.01)
     plan.when([], lambda: exchange(0, 1), ready=plan.now + 0.02)
     plan.when([], natural, ready=plan.now + 5)
+    for load in loads[2:]:
+        load.start()
     plan.run()
     for m in plan.sent:
         m.copy.wait_send()
     for s in range(2):
         for q in range(2):
-            @pl.when(jnp.logical_not(jnp.logical_and(diagonal, h == q)))
-            def _():
-                turn(s, q, 0).wait_send()
-
-
-def store(a, b, c, a_out, b_out, c_out):
-    a_out[...] = a[...]
-    b_out[...] = b[...]
-    c_out[...] = c[...]
+            turn(s, q, 0).wait_send()
+
+
+def store(a, b, c, a_out, b_out, c_out, sems):
+    copies = [
+        pltpu.make_async_copy(src, dst, sems.at[n])
+        for n, (src, dst) in enumerate(((a, a_out), (b, b_out), (c, c_out)))
+    ]
+    for cp in copies:
+        cp.start()
+    for cp in copies:
+        cp.wait()
 
 
 def shards(acts, grads, basis, moment, second):
@@ -528,11 +546,7 @@
     hbm = pl.BlockSpec(memory_space=pltpu.HBM)
     results = pl.pallas_call(
         kernel,
-        out_shape=(
-            jax.ShapeDtypeStruct(moment.shape, F32),
-            jax.ShapeDtypeStruct(second.shape, F32),
-            jax.ShapeDtypeStruct((256, 896), BF16),
-        ),
+        out_shape=(pltpu.VMEM(moment.shape, F32), pltpu.VMEM(second.shape, F32), pltpu.VMEM((256, 896), BF16)),
         in_specs=[hbm] * 5,
         out_specs=(vmem, vmem, vmem),
         scratch_shapes=[
@@ -557,25 +571,28 @@
             pltpu.VMEM((8, Q, TOK), BF16),
             pltpu.VMEM((2, 8, 2 * KEPT, TOK), BF16),
             pltpu.VMEM((2, 2 * KEPT, COLS), F32),
-            pltpu.VMEM((2, 2 * KEPT, COLS), BF16),
-            pltpu.VMEM((2, 16, R, COLS), BF16),
-            pltpu.VMEM((2, R, COLS), BF16),
-            pltpu.VMEM((2, 2, 2, 128, COLS), BF16),
+            pltpu.VMEM((2, 2 * KEPT, WIDE), BF16),
+            pltpu.VMEM((2, 16, R, WIDE), BF16),
+            pltpu.VMEM((2, 8, R, WIDE), BF16),
+            pltpu.VMEM((2, R, WIDE), BF16),
+            pltpu.VMEM((2, 2, 2, 128, WIDE), BF16),
             pltpu.VMEM((2, 256, COLS), F32),
             pltpu.SemaphoreType.DMA((5,)),
             pltpu.SemaphoreType.DMA((2 * COUNT,)),
             pltpu.SemaphoreType.DMA((2 * COUNT,)),
         ],
         compiler_params=pltpu.CompilerParams(
-            collective_id=0, has_side_effects=True, vmem_limit_bytes=60 * 2**20
+            collective_id=0, has_side_effects=True, vmem_limit_bytes=32 * 2**20
         ),
-    )(acts, basis, grads.T, moment, second)
+    )(*(pltpu.with_memory_space_constraint(a, pltpu.HBM) for a in (acts, basis, grads.T, moment, second)))
     return pl.pallas_call(
         store,
         out_shape=tuple(jax.ShapeDtypeStruct(r.shape, r.dtype) for r in results),
         in_specs=[vmem] * 3,
-        out_specs=(vmem,) * 3,
-    )(*results)
+        out_specs=(pl.BlockSpec(memory_space=pl.ANY),) * 3,
+        scratch_shapes=[pltpu.SemaphoreType.DMA((3,))],
+        compiler_params=pltpu.CompilerParams(vmem_limit_bytes=2**21),
+    )(*(pltpu.with_memory_space_constraint(r, pltpu.VMEM) for r in results))
 
 
 def solution(mesh):

time: 84.8 us -> 78.7 us (0.928)
  Pallas kernels: 83.4 us -> 77.9 us
    pallas_call x1, Pallas kernels: 81.5 us -> 77.1 us  [shards(): pl.pallas_call(kernel, out_shape=(pltpu.VMEM(moment.shape, F32), pltpu.VM...]
    pallas_call x1, Pallas kernels: 1.91 us -> 0.84 us  [shards(): pl.pallas_call(store, out_shape=tuple((jax.ShapeDtypeStruct(r.shape, r.dt...]
where the time goes in v3:
time: 78.7 us; the launch traced here: 78.6 us
  Pallas kernels  77.9 us (99%)
    pallas_call x1, Pallas kernels, shards(): pl.pallas_call(kernel, out_shape=(pltpu.VMEM(moment.shape, F32), pltpu.VM...  77.1 us

profile of v3, /device:TPU:7, one launch (start us, length us, event | category | flops | bytes accessed | tf_op | source)
XLA Modules:
  0.0 78.6 jit_solution(18371843940873376273)
XLA Ops:
  0.6 77.1 %shard_map.76 = (f32[32,448]{1,0:T(8,128)S(1)}, f32[32,448]{1,0:T(8,128)S(1)}, bf16[256,896]{1,0:T(8,128)(2,1)S(1)}) custom-call(bf16[256,2048]{1,0:T(8,128)(2,1)} %acts_hbm.1, bf16[256,512]{1,0:T(8,128)(2,1)} %basis_hbm.1, bf16[448,2048]{1,0:T(8,128)(2,1)} %bitcast.1, f32[32,448]{1,0:T(8,128)} %moment_hbm.1, f32[32,448]{1,0:T(8,128)} %second_hbm.1), custom_call_target="tpu_custom_call" | custom-call | tf_op jit(solution)/shard_map/pallas_call | solution.py:547
  77.7 0.8 %shard_map.77 = (f32[32,448]{1,0:T(8,128)}, f32[32,448]{1,0:T(8,128)}, bf16[256,896]{1,0:T(8,128)(2,1)}) custom-call(f32[32,448]{1,0:T(8,128)S(1)} %get-tuple-element.6.a, f32[32,448]{1,0:T(8,128)S(1)} %get-tuple-element.7.b, bf16[256,896]{1,0:T(8,128)(2,1)S(1)} %get-tuple-element.8.c), custom_call_target="tpu_custom_call" | custom-call | tf_op jit(solution)/shard_map/pallas_call | solution.py:588

commit v4 on v3

--- a/solution.py
+++ b/solution.py
@@ -29,7 +29,7 @@
 STEP = 58
 SHST = 66
 RELAY = 75
-COUNT = 83
+COUNT = 84
 
 
 class Message:
@@ -58,7 +58,7 @@
         for link, hops in path:
             self.free[link] = max(self.free.get(link, 0.0), self.now) + each * hops
         self.spend(0.03)
-        return start + each + 1.95 + 0.6 * sum(hops for _, hops in path)
+        return start + each + 2.6 + 0.6 * sum(hops for _, hops in path)
 
     def when(self, messages, action, ready=0.0):
         ready = max([ready] + [m.arrival for m in messages])
@@ -136,23 +136,25 @@
     def zlink(direction):
         return "z-" if direction == 0 else "z+"
 
-    def partial(s, n):
+    def partial(n):
         k = ORDER[n]
         tok = pl.ds(pl.multiple_of(((z + k) % 8) * TOK, TOK), TOK)
-        both = jnp.dot(lhs[s].reshape(2 * KEPT, 256), acts[:, tok], preferred_element_type=F32)
-        csend[s, n] = both[:KEPT].astype(BF16)
-        own[s, n] = both[KEPT:]
-        plan.spend(0.15)
-
-    def exchange(s, part):
+        product = jnp.dot(lhs[...].reshape(4 * KEPT, 256), acts[:, tok], preferred_element_type=F32)
+        for s in range(2):
+            csend[s, n] = product[s * 2 * KEPT : s * 2 * KEPT + KEPT].astype(BF16)
+            own[s, n] = product[s * 2 * KEPT + KEPT : s * 2 * KEPT + 2 * KEPT]
+        plan.spend(0.25)
+
+    def exchange(part):
         first, last = ((0, 3), (3, 8))[part]
         for n in range(first, last):
-            partial(s, n)
-        if s == 1 and part == 0:
+            partial(n)
+        if part == 0:
             pl.semaphore_wait(barrier, 14)
         place = pl.ds(first, last - first)
-        m = send(s, csend.at[s, place], crecv.at[s, place], CORE + part, at(dc=1), None, 64 * (last - first))
-        plan.when([m], lambda: ((pair_first, pair_rest), (reduce_start, reduce_rest))[s][part](s))
+        for s in (1, 0):
+            m = send(s, csend.at[s, place], crecv.at[s, place], CORE + part, at(dc=1), None, 64 * (last - first))
+            plan.when([m], lambda s=s: ((pair_first, pair_rest), (reduce_start, reduce_rest))[s][part](s))
 
     def added(s, k, half):
         n = ORDER.index(k % 8)
@@ -317,17 +319,30 @@
             m = send(s, ref, ref, GATH + number, at(dz), [(link, abs(dz))], 32 if half is None else 16)
             plan.when([m], action)
 
+        def cross(number, k, dz, action, half=None):
+            ref = fpiece(s, k, half)
+            path = [(zlink(0 if dz < 0 else 1), abs(dz)), ("x", 1), ("x2", 1)]
+            m = send(s, ref, ref, RELAY + number, at(dz, dh=1), path, 32 if half is None else 16)
+            plan.when([m], action)
+
         def farthest():
-            counted("farthest", 2, lambda: relay(4))
+            counted("farthest", 2, lambda: arrived_piece(s, 4))
+
+        def crossed():
+            counted("crossed", 2, lambda: arrived_piece(s, 4))
 
         def from_above():
             pass_on(4, 2, -2, farthest, 0)
-            pass_on(6, 2, -1, lambda: relay(3))
+            cross(4, 2, -2, crossed, 0)
+            pass_on(6, 2, -1, lambda: arrived_piece(s, 3))
+            cross(3, 2, -1, lambda: arrived_piece(s, 3))
             relay(2)
 
         def from_below():
             pass_on(5, -2, 2, farthest, 1)
-            pass_on(7, -2, 1, lambda: relay(-3))
+            cross(8, -2, 2, crossed, 1)
+            pass_on(7, -2, 1, lambda: arrived_piece(s, -3))
+            cross(5, -2, 1, lambda: arrived_piece(s, -3))
             relay(-2)
 
         pass_on(0, 0, -2, from_above)
@@ -515,10 +530,8 @@
             for half in range(2):
                 dense[:, half * COLS : half * COLS + COLS] = wide[half].astype(BF16)
 
-    exchange(1, 0)
-    plan.when([], lambda: exchange(0, 0), ready=plan.now)
-    plan.when([], lambda: exchange(1, 1), ready=plan.now + 0.01)
-    plan.when([], lambda: exchange(0, 1), ready=plan.now + 0.02)
+    exchange(0)
+    plan.when([], lambda: exchange(1), ready=plan.now)
     plan.when([], natural, ready=plan.now + 5)
     for load in loads[2:]:
         load.start()

time: 78.7 us -> 77.1 us (0.980); the launches traced: 78.6 us -> 76 us
  Pallas kernels: 77.9 us -> 75.3 us
    pallas_call x1, Pallas kernels: 77.1 us -> 74.5 us  [shards(): pl.pallas_call(kernel, out_shape=(pltpu.VMEM(moment.shape, F32), pltpu.VM...]
where the time goes in v4:
time: 77.1 us; the launch traced here: 76 us
  Pallas kernels  75.3 us (98%)
    pallas_call x1, Pallas kernels, shards(): pl.pallas_call(kernel, out_shape=(pltpu.VMEM(moment.shape, F32), pltpu.VM...  74.5 us

profile of v4, /device:TPU:7, one launch (start us, length us, event | category | flops | bytes accessed | tf_op | source)
XLA Modules:
  0.0 76.0 jit_solution(17689509601456127465)
XLA Ops:
  0.6 74.5 %shard_map.76 = (f32[32,448]{1,0:T(8,128)S(1)}, f32[32,448]{1,0:T(8,128)S(1)}, bf16[256,896]{1,0:T(8,128)(2,1)S(1)}) custom-call(bf16[256,2048]{1,0:T(8,128)(2,1)} %acts_hbm.1, bf16[256,512]{1,0:T(8,128)(2,1)} %basis_hbm.1, bf16[448,2048]{1,0:T(8,128)(2,1)} %bitcast.1, f32[32,448]{1,0:T(8,128)} %moment_hbm.1, f32[32,448]{1,0:T(8,128)} %second_hbm.1), custom_call_target="tpu_custom_call" | custom-call | tf_op jit(solution)/shard_map/pallas_call | solution.py:560
  75.1 0.8 %shard_map.77 = (f32[32,448]{1,0:T(8,128)}, f32[32,448]{1,0:T(8,128)}, bf16[256,896]{1,0:T(8,128)(2,1)}) custom-call(f32[32,448]{1,0:T(8,128)S(1)} %get-tuple-element.6.a, f32[32,448]{1,0:T(8,128)S(1)} %get-tuple-element.7.b, bf16[256,896]{1,0:T(8,128)(2,1)S(1)} %get-tuple-element.8.c), custom_call_target="tpu_custom_call" | custom-call | tf_op jit(solution)/shard_map/pallas_call | solution.py:601

commit v5 on v4

--- a/solution.py
+++ b/solution.py
@@ -29,7 +29,8 @@
 STEP = 58
 SHST = 66
 RELAY = 75
-COUNT = 84
+MORE = 84
+COUNT = 86
 
 
 class Message:
@@ -493,17 +494,27 @@
             plan.when([m], action)
 
         def from_above():
-            pass_on(4, 2, -2, lambda: hand(7, 4, 0), 0)
             pass_on(6, 2, -1, lambda: hand(5, 3))
             hand(1, 2)
 
         def from_below():
-            pass_on(5, -2, 2, lambda: hand(8, 4, 1), 1)
             pass_on(7, -2, 1, lambda: hand(6, -3))
             hand(2, -2)
 
-        pass_on(0, 0, -2, from_above)
-        pass_on(1, 0, 2, from_below)
+        def half_above(first):
+            if first:
+                pass_on(4, 2, -2, lambda: hand(7, 4, 0), 0)
+            counted(("above", s), 2, from_above)
+
+        def half_below(first):
+            if first:
+                pass_on(5, -2, 2, lambda: hand(8, 4, 1), 1)
+            counted(("below", s), 2, from_below)
+
+        pass_on(0, 0, -2, lambda: half_above(True), 0)
+        pass_on(1, 0, 2, lambda: half_below(True), 1)
+        pass_on(MORE - STEP, 0, -2, lambda: half_above(False), 1)
+        pass_on(MORE - STEP + 1, 0, 2, lambda: half_below(False), 0)
         pass_on(2, 0, -1, lambda: hand(3, 1))
         pass_on(3, 0, 1, lambda: hand(4, -1))
         hand(0, 0)

time: 77.1 us -> 77 us (level)
  no operation moved by 1% of the time
where the time goes in v5:
time: 77 us; the launch traced here: 75.9 us
  Pallas kernels  75.3 us (98%)
    pallas_call x1, Pallas kernels, shards(): pl.pallas_call(kernel, out_shape=(pltpu.VMEM(moment.shape, F32), pltpu.VM...  74.5 us

profile of v5, /device:TPU:7, one launch (start us, length us, event | category | flops | bytes accessed | tf_op | source)
XLA Modules:
  0.0 75.9 jit_solution(2755814587381949031)
XLA Ops:
  0.6 74.5 %shard_map.76 = (f32[32,448]{1,0:T(8,128)S(1)}, f32[32,448]{1,0:T(8,128)S(1)}, bf16[256,896]{1,0:T(8,128)(2,1)S(1)}) custom-call(bf16[256,2048]{1,0:T(8,128)(2,1)} %acts_hbm.1, bf16[256,512]{1,0:T(8,128)(2,1)} %basis_hbm.1, bf16[448,2048]{1,0:T(8,128)(2,1)} %bitcast.1, f32[32,448]{1,0:T(8,128)} %moment_hbm.1, f32[32,448]{1,0:T(8,128)} %second_hbm.1), custom_call_target="tpu_custom_call" | custom-call | tf_op jit(solution)/shard_map/pallas_call | solution.py:571
  75.1 0.8 %shard_map.77 = (f32[32,448]{1,0:T(8,128)}, f32[32,448]{1,0:T(8,128)}, bf16[256,896]{1,0:T(8,128)(2,1)}) custom-call(f32[32,448]{1,0:T(8,128)S(1)} %get-tuple-element.6.a, f32[32,448]{1,0:T(8,128)S(1)} %get-tuple-element.7.b, bf16[256,896]{1,0:T(8,128)(2,1)S(1)} %get-tuple-element.8.c), custom_call_target="tpu_custom_call" | custom-call | tf_op jit(solution)/shard_map/pallas_call | solution.py:612
